TPU v7x, 32 devices: a whole 2x2x4 slice. The times are simulated.
32 devices in a mesh: groups: 2 (over x), blk: 16 (over z, y, core).
Axes of the slice: x: 2, y: 2, z: 4, core: 2. Of those that a mesh axis runs over, the one named last changes fastest.
Arguments:
- flow: float32 [16384, 2560], P(('groups', 'blk')), parts along dimension 0, as said below
- occupancy: int32 [32, 5], P(('groups', 'blk')), parts along dimension 0, may hold values from 0 to 1, as said below
Outputs:
- clustered: float32 [16384, 2560], P(('groups', 'blk')), parts along dimension 0
There are 2 independent parts, one for each index of `groups`. A program takes and returns all parts, laid end to end along the dimension named above; each array names one. Nothing has to cross between parts.
Inputs may be any that keep to these rules, and one draw needn't show every extreme that they name: `occupancy`: slot 2 (the diagonal tile) of every row block is occupied; some row blocks have every slot occupied. `flow`: entries are positive.
All inputs are finite; a program needn't handle non-finite values.
Results may differ from a plain program's by a relative error of at most 0.0003.
Values sent between devices are 32-bit elements; how exact they have to be, the bound alone decides.
A program may use at most 64 MiB of HBM per device.

v0:
```python
import jax
import jax.numpy as jnp
from jax import lax
from jax.sharding import PartitionSpec as P


def shifted(value, axis, steps):
    count = lax.axis_size(axis)
    pairs = [(source, (source + steps) % count) for source in range(count)]
    return lax.ppermute(value, axis, pairs)


def fetch_rows(masked, offset, lower, upper, width):
    arrived = shifted(masked, "blk", -offset)
    return arrived[:, lower * width : upper * width]


def per_device(flow, occupancy):
    width = flow.shape[0]
    span = flow.shape[1] // width
    reach = span // 2
    slot_mask = jnp.repeat(occupancy[0].astype(jnp.float32), width)[None, :]
    masked = flow * slot_mask
    total = jnp.zeros((width, span * width), jnp.float32)
    for offset in range(-reach, reach + 1):
        lower = max(0, -offset)
        upper = min(span, span - offset)
        left = masked[:, (offset + reach) * width : (offset + reach + 1) * width]
        if offset == 0:
            window = masked
        else:
            window = fetch_rows(masked, offset, lower, upper, width)
        term = jnp.dot(
            left, window, precision=lax.Precision.HIGHEST, preferred_element_type=jnp.float32
        )
        total = total.at[:, (lower + offset) * width : (upper + offset) * width].add(term)
    expanded = total * slot_mask
    inflated = expanded * expanded
    partial_cols = jnp.sum(inflated.reshape(width, span, width), axis=0)
    column = partial_cols[reach]
    for target in range(-reach, reach + 1):
        if target != 0:
            column = column + shifted(partial_cols[target + reach], "blk", target)
    pieces = []
    for target in range(-reach, reach + 1):
        if target == 0:
            pieces.append(column)
        else:
            pieces.append(shifted(column, "blk", -target))
    near = jnp.stack(pieces, axis=0)
    return width * inflated / near.reshape(1, span * width)


def solution(mesh):
    placed = (P(("groups", "blk"), None), P(("groups", "blk"), None))
    return jax.shard_map(
        per_device,
        mesh=mesh,
        in_specs=placed,
        out_specs=P(("groups", "blk"), None),
        check_vma=False,
    )
```

profile of v0, /device:TPU:0, one launch (start us, length us, event | category | flops | bytes accessed | tf_op | source)
XLA Modules:
  0.0 403.9 jit_solution(10367932711322766892)
XLA Ops:
  0.0 0.7 convert_bitcast_fusion
  0.7 3.0 broadcast_multiply_fusion
  3.7 3.0 collective-permute-start
  6.8 4.4 %collective-permute-start.2 = (f32[512,2560]{1,0:T(8,128)S(1)}, f32[512,2560]{1,0:T(8,128)S(1)}, u32[]{:S(2)}, u32[]{:S(2)}) collective-permute-start(f32[512,2560]{1,0:T(8,128)S(1)} %broadcast_multiply_fusion), channel_id=1, source_target_pairs={{0,15},{1,0},{2,1},{3,2},{4,3},{5,4},{6,5},{7,6},{8,7},{9,8},{10,9... | collective-permute-start | bytes 15728648 | tf_op jit(solution)/shard_map/ppermute | solution.py:10
  11.6 0.6 compare_reduce_fusion.1
  12.2 0.7 compare_reduce_fusion
  13.0 275.8 %collective-permute-done = f32[512,2560]{1,0:T(8,128)S(1)} collective-permute-done((f32[512,2560]{1,0:T(8,128)S(1)}, f32[512,2560]{1,0:T(8,128)S(1)}, u32[]{:S(2)}, u32[]{:S(2)}) %collective-permute-start) | collective-permute-done | bytes 5242912 | tf_op jit(solution)/shard_map/ppermute | solution.py:10
  288.7 5.9 %convolution_select_fusion = f32[512,1536]{1,0:T(8,128)S(1)} fusion(f32[512,2560]{1,0:T(8,128)S(1)} %collective-permute-done, pred[]{:T(512)} %compare_reduce_fusion.1, f32[512,2560]{1,0:T(8,128)S(1)} %broadcast_multiply_fusion), kind=kOutput, calls=%fused_computation.11 | convolution fusion | flops 4832624640 | bytes 7340033 | tf_op jit(solution)/shard_map/dot_general | solution.py:33
  294.6 0.6 scatter-add.14
  295.3 8.5 %fusion.1 = f32[512,2560]{1,0:T(8,128)S(1)} fusion(f32[512,2560]{1,0:T(8,128)S(1)} %scatter-add.14, pred[]{:T(512)} %compare_reduce_fusion, f32[512,2560]{1,0:T(8,128)S(1)} %collective-permute-done.1, f32[512,2560]{1,0:T(8,128)S(1)} %broadcast_multiply_fusion), kind=kOutput, calls=%fused_computation.5 | convolution fusion | flops 6444548096 | bytes 13631489 | tf_op jit(solution)/shard_map/dot_general | solution.py:33
  303.8 9.0 %convolution_add_fusion = f32[512,2560]{1,0:T(8,128)S(1)} fusion(f32[512,2560]{1,0:T(8,128)S(1)} %fusion.1, f32[512,2560]{1,0:T(8,128)S(1)} %broadcast_multiply_fusion), kind=kOutput, calls=%fused_computation.3 | convolution fusion | flops 8054374400 | bytes 16777216 | tf_op jit(solution)/shard_map/dot_general | solution.py:33
  312.8 8.0 %constant_dynamic-update-slice_fusion = (f32[512,2560]{1,0:T(8,128)S(1)}, f32[512,2048]{1,0:T(8,128)S(1)}) fusion(f32[512,2560]{1,0:T(8,128)S(1)} %convolution_add_fusion, f32[512,2560]{1,0:T(8,128)S(1)} %collective-permute-done.2, f32[512,2560]{1,0:T(8,128)S(1)} %broadcast_multiply_fusion), kind=kOutput, calls=%fused_computation.29 | convolution fusion | flops 6443499520 | bytes 17825792 | tf_op jit(solution)/shard_map/dot_general | solution.py:33
  320.8 26.8 %collective-permute-done.3 = f32[512,2560]{1,0:T(8,128)S(1)} collective-permute-done((f32[512,2560]{1,0:T(8,128)S(1)}, f32[512,2560]{1,0:T(8,128)S(1)}, u32[]{:S(2)}, u32[]{:S(2)}) %collective-permute-start.3) | collective-permute-done | bytes 5242912 | tf_op jit(solution)/shard_map/ppermute | solution.py:10
  347.5 5.3 %fusion.10 = f32[512,2560]{1,0:T(8,128)S(1)} fusion(f32[512,2560]{1,0:T(8,128)S(1)} %get-tuple-element.77, f32[512,2048]{1,0:T(8,128)S(1)} %get-tuple-element.78, f32[512,2560]{1,0:T(8,128)S(1)} %collective-permute-done.3, f32[512,2560]{1,0:T(8,128)S(1)} %broadcast_multiply_fusion), kind=kOutput, calls=%fused_computation.15 | convolution fusion | flops 4832624640 | bytes 10485760 | tf_op jit(solution)/shard_map/dot_general | solution.py:33
  352.9 2.3 copy-done
  355.3 0.7 fusion
  355.9 27.3 %collective-permute-start.4 = (f32[512]{0:T(512)S(1)}, f32[512]{0:T(512)S(1)}, u32[]{:S(2)}, u32[]{:S(2)}) collective-permute-start(f32[512]{0:T(512)S(1)} %get-tuple-element.73), channel_id=1, source_target_pairs={{0,14},{1,15},{2,0},{3,1},{4,2},{5,3},{6,4},{7,5},{8,6},{9,7},{10,... | collective-permute-start | bytes 6152 | tf_op jit(solution)/shard_map/ppermute | solution.py:10
  383.8 0.8 collective-permute-done.4
  384.6 4.4 %collective-permute-done.6 = f32[512]{0:T(512)S(1)} collective-permute-done((f32[512]{0:T(512)S(1)}, f32[512]{0:T(512)S(1)}, u32[]{:S(2)}, u32[]{:S(2)}) %collective-permute-start.6) | collective-permute-done | bytes 2080 | tf_op jit(solution)/shard_map/ppermute | solution.py:10
  389.0 1.1 collective-permute-done.7
  390.1 4.4 %collective-permute-start.10 = (f32[512]{0:T(512)S(1)}, f32[512]{0:T(512)S(1)}, u32[]{:S(2)}, u32[]{:S(2)}) collective-permute-start(f32[512]{0:T(512)S(1)} %fusion.27), channel_id=1, source_target_pairs={{0,15},{1,0},{2,1},{3,2},{4,3},{5,4},{6,5},{7,6},{8,7},{9,8},{10,9... | collective-permute-start | bytes 6152 | tf_op jit(solution)/shard_map/ppermute | solution.py:10
  394.6 2.0 collective-permute-start.11
  396.5 1.6 collective-permute-done.11
  398.2 5.8 %multiply_divide_fusion = f32[512,2560]{1,0:T(8,128)} fusion(f32[512,2560]{1,0:T(8,128)} %copy-done, f32[2560]{0:T(1024)S(1)} %div.10, f32[2560]{0:T(1024)S(1)} %mul.25), kind=kLoop, calls=%fused_computation.1 | loop fusion | flops 5242880 | bytes 10506240 | tf_op jit(solution)/shard_map/div | solution.py:51
  (20 shorter events, 1.1 us)
Async XLA Ops:
  3.7 285.0 %collective-permute-start = (f32[512,2560]{1,0:T(8,128)S(1)}, f32[512,2560]{1,0:T(8,128)S(1)}, u32[]{:S(2)}, u32[]{:S(2)}) collective-permute-start(f32[512,2560]{1,0:T(8,128)S(1)} %broadcast_multiply_fusion), channel_id=1, source_target_pairs={{0,2},{1,3},{2,4},{3,5},{4,6},{5,7},{6,8},{7,9},{8,10},{9,11},{10,... | collective-permute-start | bytes 15728648 | tf_op jit(solution)/shard_map/ppermute | solution.py:10
  6.8 288.5 %collective-permute-start.1 = (f32[512,2560]{1,0:T(8,128)S(1)}, f32[512,2560]{1,0:T(8,128)S(1)}, u32[]{:S(2)}, u32[]{:S(2)}) collective-permute-start(f32[512,2560]{1,0:T(8,128)S(1)} %broadcast_multiply_fusion), channel_id=1, source_target_pairs={{0,1},{1,2},{2,3},{3,4},{4,5},{5,6},{6,7},{7,8},{8,9},{9,10},{10,1... | collective-permute-start | bytes 15728648 | tf_op jit(solution)/shard_map/ppermute | solution.py:10
  6.8 306.1 %collective-permute-start.2 = (f32[512,2560]{1,0:T(8,128)S(1)}, f32[512,2560]{1,0:T(8,128)S(1)}, u32[]{:S(2)}, u32[]{:S(2)}) collective-permute-start(f32[512,2560]{1,0:T(8,128)S(1)} %broadcast_multiply_fusion), channel_id=1, source_target_pairs={{0,15},{1,0},{2,1},{3,2},{4,3},{5,4},{6,5},{7,6},{8,7},{9,8},{10,9... | collective-permute-start | bytes 15728648 | tf_op jit(solution)/shard_map/ppermute | solution.py:10
  11.2 336.3 %collective-permute-start.3 = (f32[512,2560]{1,0:T(8,128)S(1)}, f32[512,2560]{1,0:T(8,128)S(1)}, u32[]{:S(2)}, u32[]{:S(2)}) collective-permute-start(f32[512,2560]{1,0:T(8,128)S(1)} %broadcast_multiply_fusion), channel_id=1, source_target_pairs={{0,14},{1,15},{2,0},{3,1},{4,2},{5,3},{6,4},{7,5},{8,6},{9,7},{10,... | collective-permute-start | bytes 15728648 | tf_op jit(solution)/shard_map/ppermute | solution.py:10
  352.9 2.4 copy-start
  355.9 28.7 %collective-permute-start.4 = (f32[512]{0:T(512)S(1)}, f32[512]{0:T(512)S(1)}, u32[]{:S(2)}, u32[]{:S(2)}) collective-permute-start(f32[512]{0:T(512)S(1)} %get-tuple-element.73), channel_id=1, source_target_pairs={{0,14},{1,15},{2,0},{3,1},{4,2},{5,3},{6,4},{7,5},{8,6},{9,7},{10,... | collective-permute-start | bytes 6152 | tf_op jit(solution)/shard_map/ppermute | solution.py:10
  383.3 1.3 collective-permute-start.5
  383.3 5.7 %collective-permute-start.6 = (f32[512]{0:T(512)S(1)}, f32[512]{0:T(512)S(1)}, u32[]{:S(2)}, u32[]{:S(2)}) collective-permute-start(f32[512]{0:T(512)S(1)} %get-tuple-element.75), channel_id=1, source_target_pairs={{0,1},{1,2},{2,3},{3,4},{4,5},{5,6},{6,7},{7,8},{8,9},{9,10},{10,1... | collective-permute-start | bytes 6152 | tf_op jit(solution)/shard_map/ppermute | solution.py:10
  383.8 6.3 %collective-permute-start.7 = (f32[512]{0:T(512)S(1)}, f32[512]{0:T(512)S(1)}, u32[]{:S(2)}, u32[]{:S(2)}) collective-permute-start(f32[512]{0:T(512)S(1)} %get-tuple-element.74), channel_id=1, source_target_pairs={{0,2},{1,3},{2,4},{3,5},{4,6},{5,7},{6,8},{7,9},{8,10},{9,11},{10,... | collective-permute-start | bytes 6152 | tf_op jit(solution)/shard_map/ppermute | solution.py:10
  390.1 6.5 %collective-permute-start.8 = (f32[512]{0:T(512)S(1)}, f32[512]{0:T(512)S(1)}, u32[]{:S(2)}, u32[]{:S(2)}) collective-permute-start(f32[512]{0:T(512)S(1)} %fusion.27), channel_id=1, source_target_pairs={{0,2},{1,3},{2,4},{3,5},{4,6},{5,7},{6,8},{7,9},{8,10},{9,11},{10,... | collective-permute-start | bytes 6152 | tf_op jit(solution)/shard_map/ppermute | solution.py:10
  390.1 6.5 %collective-permute-start.9 = (f32[512]{0:T(512)S(1)}, f32[512]{0:T(512)S(1)}, u32[]{:S(2)}, u32[]{:S(2)}) collective-permute-start(f32[512]{0:T(512)S(1)} %fusion.27), channel_id=1, source_target_pairs={{0,1},{1,2},{2,3},{3,4},{4,5},{5,6},{6,7},{7,8},{8,9},{9,10},{10,1... | collective-permute-start | bytes 6152 | tf_op jit(solution)/shard_map/ppermute | solution.py:10
  390.1 6.4 %collective-permute-start.10 = (f32[512]{0:T(512)S(1)}, f32[512]{0:T(512)S(1)}, u32[]{:S(2)}, u32[]{:S(2)}) collective-permute-start(f32[512]{0:T(512)S(1)} %fusion.27), channel_id=1, source_target_pairs={{0,15},{1,0},{2,1},{3,2},{4,3},{5,4},{6,5},{7,6},{8,7},{9,8},{10,9... | collective-permute-start | bytes 6152 | tf_op jit(solution)/shard_map/ppermute | solution.py:10
  394.6 3.6 collective-permute-start.11
where the time goes:
time: 404 us
  waiting for transfers between devices  310 us (77%)
  starting transfers between devices  42.2 us (10%)
  matrix products  36.7 us (9%)
  other arithmetic  11.4 us (3%)
    ppermute x12, waiting for transfers between devices, shifted(): return lax.ppermute(value, axis, pairs)  310 us
    ppermute x12, starting transfers between devices, shifted(): return lax.ppermute(value, axis, pairs)  42.2 us
    dot_general x5, matrix products, per_device(): jnp.dot(left, window, precision=lax.Precision.HIGHEST, preferred_element_...  36.7 us
  transfers between devices with their start and end apart: 12, of which 6 were waited for; matrix products, arithmetic and copies ran while one was open for 8% of the time, Pallas kernels for 0%

commit v1 on v0

v1 whole, which is shorter than its diff:
```python
import functools

import jax
import jax.numpy as jnp
from jax import lax
from jax.experimental import pallas as pl
from jax.experimental.pallas import tpu as pltpu
from jax.sharding import PartitionSpec as P

MESH = pl.DeviceIdType.MESH
SPAN = 5
REACH = 2
NEAR = 4
WINDOW = 2


def place(offset, slot):
    return {1: 0, 2: 4, -1: 6, -2: 9}[offset] + slot


OUTER_SENDS = (
    (3, 2, place(2, 1)),
    (2, 2, place(2, 2)),
    (1, -1, place(-1, 3)),
    (0, -1, place(-1, 4)),
    (4, 2, place(2, 0)),
)
INNER_SENDS = (
    (2, 1, place(1, 2)),
    (1, 1, place(1, 3)),
    (4, 1, place(1, 0)),
    (3, 1, place(1, 1)),
    (0, -2, place(-2, 4)),
)
OUTER_STEPS = ((2, 2), (-2, 2), (-1, 1), (-2, 3), (-1, 2), (-1, 3), (2, 0), (-1, 4), (2, 1), (-2, 4))
INNER_STEPS = ((1, 2), (2, 1), (1, 3), (2, 2), (1, 0), (-2, 2), (1, 1), (-2, 3), (2, 0), (-2, 4))
OUTER_FORWARDS = {
    (-1, 2): ((1, place(-2, 2)),),
    (-1, 3): ((1, place(-2, 3)),),
    (-1, 4): ((1, place(-2, 4)),),
}
INNER_FORWARDS = {
    (1, 2): ((3, place(-2, 2)), (-1, place(2, 2))),
    (2, 1): ((3, place(-1, 1)),),
    (1, 3): ((3, place(-2, 3)),),
    (2, 2): ((3, place(-1, 2)),),
    (1, 0): ((-1, place(2, 0)),),
    (1, 1): ((-1, place(2, 1)),),
}
COMPLETE = {1: (4, 3), 3: (0, 4), 5: (1, 0), 8: (3, 1), 9: (2, 2)}
NEXT_SEND = {0: 2, 2: 3, 4: 4}


def body(
    count,
    width,
    flow_ref,
    occ_ref,
    infl_ref,
    near_ref,
    own,
    high,
    low,
    recv,
    acc,
    right_high,
    right_low,
    parts,
    load_sem,
    store_sem,
    send_sem,
    recv_sem,
    part_send_sem,
    part_recv_sem,
):
    me = lax.axis_index("blk")
    spot = lax.rem(me, 4)
    outer = jnp.logical_or(spot == 0, spot == 3)
    sign = jnp.where(spot < 2, 1, -1)

    def pick(a, b):
        return a if isinstance(a, int) and a == b else jnp.where(outer, a, b)

    def peer(offset):
        return {"blk": lax.rem(me + sign * offset + count, count)}

    def absolute(slot):
        return REACH + sign * (slot - REACH)

    def columns(slot):
        return pl.ds(pl.multiple_of(absolute(slot) * width, width), width)

    def load(slot):
        return pltpu.make_async_copy(flow_ref.at[:, columns(slot)], own.at[slot], load_sem.at[slot])

    def remote(source, target, where, sem):
        return pltpu.make_async_remote_copy(
            src_ref=source,
            dst_ref=recv.at[where],
            send_sem=send_sem.at[sem],
            recv_sem=recv_sem.at[where],
            device_id=target,
            device_id_type=MESH,
        )

    own_slots = [pick(OUTER_SENDS[t][0], INNER_SENDS[t][0]) for t in range(SPAN)]
    for t in range(SPAN):
        load(own_slots[t]).start()

    barrier = pltpu.get_barrier_semaphore()
    for distance in range(1, NEAR + 1):
        for offset in (distance, -distance):
            pl.semaphore_signal(barrier, inc=1, device_id=peer(offset), device_id_type=MESH)
    pl.semaphore_wait(barrier, 2 * NEAR)

    rows = 64

    def prepare(slot):
        load(slot).wait()
        factor = occ_ref[0, absolute(slot)].astype(jnp.float32)

        @pl.loop(0, width // rows)
        def _(r):
            at = pl.ds(pl.multiple_of(r * rows, rows), rows)
            masked = own[slot, at, :] * factor
            own[slot, at, :] = masked
            top = masked.astype(jnp.bfloat16)
            high[slot, at, :] = top
            low[slot, at, :] = (masked - top.astype(jnp.float32)).astype(jnp.bfloat16)

    def send(t):
        source, offset, where = (pick(a, b) for a, b in zip(OUTER_SENDS[t], INNER_SENDS[t]))
        return remote(own.at[source], peer(offset), where, t)

    def local_send(q):
        return remote(own.at[pick(q + 1, q)], peer(pick(1, -1)), pick(place(-1, q + 1), place(1, q)), SPAN + q)

    for t in range(SPAN):
        prepare(own_slots[t])
        if t < WINDOW:
            send(t).start()
    for q in range(SPAN - 1):
        local_send(q).start()

    half = width // 2

    def multiply(left, get_high, get_low, out, first):
        @pl.loop(0, 2)
        def _(c):
            at = pl.ds(pl.multiple_of(c * half, half), half)
            term = functools.partial(jnp.dot, preferred_element_type=jnp.float32)
            total = term(high[left], get_high(at))
            total += term(high[left], get_low(at)) + term(low[left], get_high(at))
            if first:
                acc[out, :, at] = total
            else:
                acc[out, :, at] += total

    @pl.loop(0, SPAN)
    def _(slot):
        multiply(REACH, lambda at: high[slot, :, at], lambda at: low[slot, :, at], slot, True)

    def arrived(where):
        remote(recv.at[where], peer(1), where, 0).wait_recv()

    def add(where, left, out):
        @pl.loop(0, width // rows)
        def _(r):
            at = pl.ds(pl.multiple_of(r * rows, rows), rows)
            value = recv[where, at, :]
            top = value.astype(jnp.bfloat16)
            right_high[at, :] = top
            right_low[at, :] = (value - top.astype(jnp.float32)).astype(jnp.bfloat16)

        multiply(left, lambda at: right_high[:, at], lambda at: right_low[:, at], out, False)

    @pl.loop(0, SPAN - 1)
    def _(q):
        where = jnp.where(outer, q, place(-1, 1) + q)
        arrived(where)
        add(where, pick(3, 1), jnp.where(outer, q + 1, q))

    def store(slot):
        return pltpu.make_async_copy(acc.at[slot], infl_ref.at[:, columns(slot)], store_sem.at[slot])

    parts[NEAR] = jnp.zeros((8, width), jnp.float32)

    def complete(slot):
        factor = occ_ref[0, absolute(slot)].astype(jnp.float32)

        def some(r, total):
            at = pl.ds(pl.multiple_of(r * rows, rows), rows)
            expanded = acc[slot, at, :] * factor
            inflated = expanded * expanded
            acc[slot, at, :] = inflated
            return total + jnp.sum(inflated.reshape(rows // 8, 8, width), axis=0)

        total = lax.fori_loop(0, width // rows, some, jnp.zeros((8, width), jnp.float32))
        parts[NEAR, pl.ds(absolute(slot), 1), :] = jnp.sum(total, axis=0, keepdims=True)
        store(slot).start()

    def forwards(table, tile):
        found = []
        order = [(t, f) for t in table for f in table[t]]
        for number, (t, (offset, where)) in enumerate(order):
            if t == tile:
                found.append(remote(recv.at[place(*t)], peer(offset), where, 2 * SPAN - 1 + number))
        return found

    for step in range(10):
        far, near = OUTER_STEPS[step], INNER_STEPS[step]
        if step in NEXT_SEND:
            t = NEXT_SEND[step]
            send(t - WINDOW).wait_send()
            send(t).start()
        where = pick(place(*far), place(*near))
        arrived(where)
        if far in OUTER_FORWARDS:
            @pl.when(outer)
            def _():
                for copy in forwards(OUTER_FORWARDS, far):
                    copy.start()
        if near in INNER_FORWARDS:
            @pl.when(jnp.logical_not(outer))
            def _():
                for copy in forwards(INNER_FORWARDS, near):
                    copy.start()
        add(where, pick(far[0] + REACH, near[0] + REACH), pick(sum(far), sum(near)))
        if step in COMPLETE:
            complete(pick(*COMPLETE[step]))

    def part(offset):
        target = {"blk": lax.rem(me + offset + count, count)}
        return pltpu.make_async_remote_copy(
            src_ref=parts.at[NEAR],
            dst_ref=parts.at[NEAR - offset],
            send_sem=part_send_sem.at[NEAR - offset],
            recv_sem=part_recv_sem.at[NEAR - offset],
            device_id=target,
            device_id_type=MESH,
        )

    reaches = [offset for offset in range(-NEAR, NEAR + 1) if offset != 0]
    for offset in reaches:
        part(offset).start()
    for offset in reaches:
        part(offset).wait_recv()
    for slot in range(SPAN):
        total = parts[slot, pl.ds(SPAN - 1, 1), :]
        for d in range(slot - REACH * 2 + 1, slot + 1):
            total = total + parts[NEAR + d, pl.ds(slot - d, 1), :]
        near_ref[:, slot * width : (slot + 1) * width] = total

    for offset in reaches:
        part(offset).wait_send()
    for slot in range(SPAN):
        store(slot).wait()
    for t in range(SPAN - WINDOW, SPAN):
        send(t).wait_send()
    for q in range(SPAN - 1):
        local_send(q).wait_send()

    @pl.when(outer)
    def _():
        for tile in OUTER_FORWARDS:
            for copy in forwards(OUTER_FORWARDS, tile):
                copy.wait_send()

    @pl.when(jnp.logical_not(outer))
    def _():
        for tile in INNER_FORWARDS:
            for copy in forwards(INNER_FORWARDS, tile):
                copy.wait_send()


def per_device(count, flow, occupancy):
    width = flow.shape[0]
    tile = (width, width)
    places = 14
    inflated, near = pl.pallas_call(
        functools.partial(body, count, width),
        out_shape=(
            jax.ShapeDtypeStruct(flow.shape, jnp.float32),
            jax.ShapeDtypeStruct((1, flow.shape[1]), jnp.float32),
        ),
        in_specs=[
            pl.BlockSpec(memory_space=pl.ANY),
            pl.BlockSpec(memory_space=pltpu.SMEM),
        ],
        out_specs=(
            pl.BlockSpec(memory_space=pl.ANY),
            pl.BlockSpec(memory_space=pltpu.VMEM),
        ),
        scratch_shapes=[
            pltpu.VMEM((SPAN, *tile), jnp.float32),
            pltpu.VMEM((SPAN, *tile), jnp.bfloat16),
            pltpu.VMEM((SPAN, *tile), jnp.bfloat16),
            pltpu.VMEM((places, *tile), jnp.float32),
            pltpu.VMEM((SPAN, *tile), jnp.float32),
            pltpu.VMEM(tile, jnp.bfloat16),
            pltpu.VMEM(tile, jnp.bfloat16),
            pltpu.VMEM((2 * NEAR + 1, 8, width), jnp.float32),
            pltpu.SemaphoreType.DMA((SPAN,)),
            pltpu.SemaphoreType.DMA((SPAN,)),
            pltpu.SemaphoreType.DMA((2 * SPAN - 1 + 8,)),
            pltpu.SemaphoreType.DMA((places,)),
            pltpu.SemaphoreType.DMA((2 * NEAR + 1,)),
            pltpu.SemaphoreType.DMA((2 * NEAR + 1,)),
        ],
        compiler_params=pltpu.CompilerParams(
            collective_id=0, has_side_effects=True, vmem_limit_bytes=48 * 1024 * 1024
        ),
        name="expand",
    )(flow, occupancy)
    return width * inflated / near


def solution(mesh):
    placed = (P(("groups", "blk"), None), P(("groups", "blk"), None))
    return jax.shard_map(
        functools.partial(per_device, mesh.shape["blk"]),
        mesh=mesh,
        in_specs=placed,
        out_specs=P(("groups", "blk"), None),
        check_vma=False,
    )
```

time: 404 us -> 142 us (0.35)
  waiting for transfers between devices: 310 us -> 0 us
  Pallas kernels: 0 us -> 134 us
  starting transfers between devices: 42.2 us -> 0 us
  matrix products: 36.7 us -> 0 us
  other arithmetic: 11.4 us -> 5.64 us
    ppermute x12 -> x0, waiting for transfers between devices: 310 us -> none  [shifted(): return lax.ppermute(value, axis, pairs)]
    pallas_call x0 -> x1, Pallas kernels: none -> 134 us  [per_device(): pl.pallas_call(functools.partial(body, count, width), out_shape=(jax.Shap...]
    ppermute x12 -> x0, starting transfers between devices: 42.2 us -> none  [shifted(): return lax.ppermute(value, axis, pairs)]
    dot_general x5 -> x0, matrix products: 36.7 us -> none  [per_device(): jnp.dot(left, window, precision=lax.Precision.HIGHEST, preferred_element_...]
  transfers between devices with their start and end apart: 12 -> 0, of which waited for: 6 -> 0; matrix products, arithmetic and copies ran while one was open for 8% -> 0% of each run, Pallas kernels for 0% -> 0%
where the time goes in v1:
time: 142 us
  Pallas kernels  134 us (94%)
  other arithmetic  5.64 us (4%)
  local copies, waits for them, and re-layouts  3.01 us (2%)
    pallas_call x1, Pallas kernels, per_device(): pl.pallas_call(functools.partial(body, count, width), out_shape=(jax.Shap...  134 us
    div x1, other arithmetic, per_device(): return width * inflated / near  5.61 us
    unnamed x4, local copies, waits for them, and re-layouts  3.01 us

profile of v1, /device:TPU:0, one launch (start us, length us, event | category | flops | bytes accessed | tf_op | source)
XLA Modules:
  0.0 142.2 jit_solution(13845979778559684251)
XLA Ops:
  0.0 0.0 copy-start.1
  0.0 0.7 copy-done.1
  0.7 133.5 %expand.1 = (f32[512,2560]{1,0:T(8,128)S(1)}, f32[1,2560]{1,0:T(1,128)S(1)}) custom-call(f32[512,2560]{1,0:T(8,128)} %flow_ref.1, s32[1,5]{1,0:T(1,128)S(1)} %copy-done.1), custom_call_target="tpu_custom_call" | custom-call | tf_op jit(solution)/shard_map/expand/pallas_call | solution.py:280
  134.2 0.0 copy-start
  134.2 2.3 %copy-done = f32[512,2560]{1,0:T(8,128)} copy-done((f32[512,2560]{1,0:T(8,128)}, f32[512,2560]{1,0:T(8,128)S(1)}, u32[]{:S(2)}) %copy-start) | copy-done | bytes 5242904
  136.6 5.6 %multiply_divide_fusion = f32[512,2560]{1,0:T(8,128)} fusion(f32[512,2560]{1,0:T(8,128)} %copy-done, f32[2560]{0:T(1024)S(1)} %reduce), kind=kLoop, calls=%fused_computation | loop fusion | flops 2621440 | bytes 10496000 | tf_op jit(solution)/shard_map/div | solution.py:315
  (1 shorter events, 0.0 us)
Async XLA Ops:
  0.0 0.7 copy-start.1
  134.2 2.4 %copy-start = (f32[512,2560]{1,0:T(8,128)}, f32[512,2560]{1,0:T(8,128)S(1)}, u32[]{:S(2)}) copy-start(f32[512,2560]{1,0:T(8,128)S(1)} %get-tuple-element.7) | copy-start | bytes 15728644

commit v2 on v1

--- a/solution.py
+++ b/solution.py
@@ -11,7 +11,6 @@
 SPAN = 5
 REACH = 2
 NEAR = 4
-WINDOW = 2
 
 
 def place(offset, slot):
@@ -29,11 +28,11 @@
     (2, 1, place(1, 2)),
     (1, 1, place(1, 3)),
     (4, 1, place(1, 0)),
+    (0, -2, place(-2, 4)),
     (3, 1, place(1, 1)),
-    (0, -2, place(-2, 4)),
 )
-OUTER_STEPS = ((2, 2), (-2, 2), (-1, 1), (-2, 3), (-1, 2), (-1, 3), (2, 0), (-1, 4), (2, 1), (-2, 4))
-INNER_STEPS = ((1, 2), (2, 1), (1, 3), (2, 2), (1, 0), (-2, 2), (1, 1), (-2, 3), (2, 0), (-2, 4))
+OUTER_STEPS = ((2, 2), (-2, 2), (-1, 1), (-2, 3), (-1, 2), (-1, 3), (2, 0), (-2, 4), (-1, 4), (2, 1))
+INNER_STEPS = ((1, 2), (2, 1), (1, 3), (2, 2), (1, 0), (-2, 2), (-2, 3), (1, 1), (2, 0), (-2, 4))
 OUTER_FORWARDS = {
     (-1, 2): ((1, place(-2, 2)),),
     (-1, 3): ((1, place(-2, 3)),),
@@ -47,8 +46,7 @@
     (1, 0): ((-1, place(2, 0)),),
     (1, 1): ((-1, place(2, 1)),),
 }
-COMPLETE = {1: (4, 3), 3: (0, 4), 5: (1, 0), 8: (3, 1), 9: (2, 2)}
-NEXT_SEND = {0: 2, 2: 3, 4: 4}
+COMPLETE = {1: (4, 3), 3: (0, 4), 5: (1, 0), 8: (2, 1), 9: (3, 2)}
 
 
 def body(
@@ -56,8 +54,7 @@
     width,
     flow_ref,
     occ_ref,
-    infl_ref,
-    near_ref,
+    out_ref,
     own,
     high,
     low,
@@ -67,7 +64,6 @@
     right_low,
     parts,
     load_sem,
-    store_sem,
     send_sem,
     recv_sem,
     part_send_sem,
@@ -111,8 +107,6 @@
     for distance in range(1, NEAR + 1):
         for offset in (distance, -distance):
             pl.semaphore_signal(barrier, inc=1, device_id=peer(offset), device_id_type=MESH)
-    pl.semaphore_wait(barrier, 2 * NEAR)
-
     rows = 64
 
     def prepare(slot):
@@ -137,8 +131,9 @@
 
     for t in range(SPAN):
         prepare(own_slots[t])
-        if t < WINDOW:
-            send(t).start()
+        if t == 0:
+            pl.semaphore_wait(barrier, 2 * NEAR)
+        send(t).start()
     for q in range(SPAN - 1):
         local_send(q).start()
 
@@ -180,11 +175,6 @@
         arrived(where)
         add(where, pick(3, 1), jnp.where(outer, q + 1, q))
 
-    def store(slot):
-        return pltpu.make_async_copy(acc.at[slot], infl_ref.at[:, columns(slot)], store_sem.at[slot])
-
-    parts[NEAR] = jnp.zeros((8, width), jnp.float32)
-
     def complete(slot):
         factor = occ_ref[0, absolute(slot)].astype(jnp.float32)
 
@@ -196,8 +186,7 @@
             return total + jnp.sum(inflated.reshape(rows // 8, 8, width), axis=0)
 
         total = lax.fori_loop(0, width // rows, some, jnp.zeros((8, width), jnp.float32))
-        parts[NEAR, pl.ds(absolute(slot), 1), :] = jnp.sum(total, axis=0, keepdims=True)
-        store(slot).start()
+        parts[NEAR, absolute(slot)] = jnp.sum(total, axis=0, keepdims=True)
 
     def forwards(table, tile):
         found = []
@@ -209,10 +198,6 @@
 
     for step in range(10):
         far, near = OUTER_STEPS[step], INNER_STEPS[step]
-        if step in NEXT_SEND:
-            t = NEXT_SEND[step]
-            send(t - WINDOW).wait_send()
-            send(t).start()
         where = pick(place(*far), place(*near))
         arrived(where)
         if far in OUTER_FORWARDS:
@@ -231,9 +216,10 @@
 
     def part(offset):
         target = {"blk": lax.rem(me + offset + count, count)}
+        needed = pl.ds(max(0, offset), SPAN - abs(offset))
         return pltpu.make_async_remote_copy(
-            src_ref=parts.at[NEAR],
-            dst_ref=parts.at[NEAR - offset],
+            src_ref=parts.at[NEAR, needed],
+            dst_ref=parts.at[NEAR - offset, needed],
             send_sem=part_send_sem.at[NEAR - offset],
             recv_sem=part_recv_sem.at[NEAR - offset],
             device_id=target,
@@ -246,16 +232,21 @@
     for offset in reaches:
         part(offset).wait_recv()
     for slot in range(SPAN):
-        total = parts[slot, pl.ds(SPAN - 1, 1), :]
+        total = parts[slot, SPAN - 1]
         for d in range(slot - REACH * 2 + 1, slot + 1):
-            total = total + parts[NEAR + d, pl.ds(slot - d, 1), :]
-        near_ref[:, slot * width : (slot + 1) * width] = total
+            total = total + parts[NEAR + d, slot - d]
+        scale = jnp.where(total > 1.0, 2.0**-64, 2.0**64)
+        factor = width / (total * scale)
+        source = absolute(slot)
+
+        @pl.loop(0, width // rows)
+        def _(r):
+            at = pl.ds(pl.multiple_of(r * rows, rows), rows)
+            out_ref[at, slot * width : (slot + 1) * width] = acc[source, at, :] * scale * factor
 
     for offset in reaches:
         part(offset).wait_send()
-    for slot in range(SPAN):
-        store(slot).wait()
-    for t in range(SPAN - WINDOW, SPAN):
+    for t in range(SPAN):
         send(t).wait_send()
     for q in range(SPAN - 1):
         local_send(q).wait_send()
@@ -277,20 +268,14 @@
     width = flow.shape[0]
     tile = (width, width)
     places = 14
-    inflated, near = pl.pallas_call(
+    return pl.pallas_call(
         functools.partial(body, count, width),
-        out_shape=(
-            jax.ShapeDtypeStruct(flow.shape, jnp.float32),
-            jax.ShapeDtypeStruct((1, flow.shape[1]), jnp.float32),
-        ),
+        out_shape=jax.ShapeDtypeStruct(flow.shape, jnp.float32),
         in_specs=[
             pl.BlockSpec(memory_space=pl.ANY),
             pl.BlockSpec(memory_space=pltpu.SMEM),
         ],
-        out_specs=(
-            pl.BlockSpec(memory_space=pl.ANY),
-            pl.BlockSpec(memory_space=pltpu.VMEM),
-        ),
+        out_specs=pl.BlockSpec(memory_space=pltpu.VMEM),
         scratch_shapes=[
             pltpu.VMEM((SPAN, *tile), jnp.float32),
             pltpu.VMEM((SPAN, *tile), jnp.bfloat16),
@@ -299,8 +284,7 @@
             pltpu.VMEM((SPAN, *tile), jnp.float32),
             pltpu.VMEM(tile, jnp.bfloat16),
             pltpu.VMEM(tile, jnp.bfloat16),
-            pltpu.VMEM((2 * NEAR + 1, 8, width), jnp.float32),
-            pltpu.SemaphoreType.DMA((SPAN,)),
+            pltpu.VMEM((2 * NEAR + 1, SPAN, 1, width), jnp.float32),
             pltpu.SemaphoreType.DMA((SPAN,)),
             pltpu.SemaphoreType.DMA((2 * SPAN - 1 + 8,)),
             pltpu.SemaphoreType.DMA((places,)),
@@ -312,7 +296,6 @@
         ),
         name="expand",
     )(flow, occupancy)
-    return width * inflated / near
 
 
 def solution(mesh):

time: 142 us -> 132 us (0.930)
  other arithmetic: 5.64 us -> 0 us
  Pallas kernels: 134 us -> 129 us
    div x1 -> x0, other arithmetic: 5.61 us -> none  [per_device(): return width * inflated / near]
    pallas_call x1, Pallas kernels: 134 us -> 129 us  [per_device(): pl.pallas_call(functools.partial(body, count, width), out_shape=jax.Shape...]
    unnamed x4 -> x3, local copies, waits for them, and re-layouts: 3.01 us -> 3.02 us
where the time goes in v2:
time: 132 us
  Pallas kernels  129 us (98%)
  local copies, waits for them, and re-layouts  3.02 us (2%)
    pallas_call x1, Pallas kernels, per_device(): pl.pallas_call(functools.partial(body, count, width), out_shape=jax.Shape...  129 us
    unnamed x3, local copies, waits for them, and re-layouts  3.02 us

profile of v2, /device:TPU:0, one launch (start us, length us, event | category | flops | bytes accessed | tf_op | source)
XLA Modules:
  0.0 132.2 jit_solution(15097512525729527238)
XLA Ops:
  0.0 0.0 copy-start
  0.0 0.7 copy-done
  0.7 129.2 %expand.1 = f32[512,2560]{1,0:T(8,128)S(1)} custom-call(f32[512,2560]{1,0:T(8,128)} %flow_ref.1, s32[1,5]{1,0:T(1,128)S(1)} %copy-done), custom_call_target="tpu_custom_call" | custom-call | tf_op jit(solution)/shard_map/expand/pallas_call | solution.py:271
  129.8 2.4 %copy.4 = f32[512,2560]{1,0:T(8,128)} copy(f32[512,2560]{1,0:T(8,128)S(1)} %expand.1) | data formatting | bytes 10485760
Async XLA Ops:
  0.0 0.7 copy-start

commit v3 on v2

--- a/solution.py
+++ b/solution.py
@@ -31,8 +31,8 @@
     (0, -2, place(-2, 4)),
     (3, 1, place(1, 1)),
 )
-OUTER_STEPS = ((2, 2), (-2, 2), (-1, 1), (-2, 3), (-1, 2), (-1, 3), (2, 0), (-2, 4), (-1, 4), (2, 1))
-INNER_STEPS = ((1, 2), (2, 1), (1, 3), (2, 2), (1, 0), (-2, 2), (-2, 3), (1, 1), (2, 0), (-2, 4))
+OUTER_STEPS = ((2, 2), (-2, 2), (-1, 1), (-2, 3), (-1, 2), (-1, 3), (2, 0), (-1, 4), (-2, 4), (2, 1))
+INNER_STEPS = ((1, 2), (2, 1), (1, 3), (2, 2), (1, 0), (-2, 2), (-2, 3), (-2, 4), (1, 1), (2, 0))
 OUTER_FORWARDS = {
     (-1, 2): ((1, place(-2, 2)),),
     (-1, 3): ((1, place(-2, 3)),),

time: 132 us -> 131 us (level)
  no operation moved by 1% of the time
where the time goes in v3:
time: 131 us
  Pallas kernels  128 us (98%)
  local copies, waits for them, and re-layouts  3.02 us (2%)
    pallas_call x1, Pallas kernels, per_device(): pl.pallas_call(functools.partial(body, count, width), out_shape=jax.Shape...  128 us
    unnamed x3, local copies, waits for them, and re-layouts  3.02 us

profile of v3, /device:TPU:0, one launch (start us, length us, event | category | flops | bytes accessed | tf_op | source)
XLA Modules:
  0.0 131.3 jit_solution(16626825284501751070)
XLA Ops:
  0.0 0.0 copy-start
  0.0 0.7 copy-done
  0.7 128.3 %expand.1 = f32[512,2560]{1,0:T(8,128)S(1)} custom-call(f32[512,2560]{1,0:T(8,128)} %flow_ref.1, s32[1,5]{1,0:T(1,128)S(1)} %copy-done), custom_call_target="tpu_custom_call" | custom-call | tf_op jit(solution)/shard_map/expand/pallas_call | solution.py:271
  128.9 2.4 %copy.4 = f32[512,2560]{1,0:T(8,128)} copy(f32[512,2560]{1,0:T(8,128)S(1)} %expand.1) | data formatting | bytes 10485760
Async XLA Ops:
  0.0 0.7 copy-start
